TPU v7x, 512 devices: a whole 4x8x8 slice. The times are simulated.
512 devices in a mesh: chan: 32 (over x_lo, y, core), inp: 16 (over x_hi, z).
Axes of the slice: x: 4 (x_hi: 2, x_lo: 2; x = x_hi * 2 + x_lo), y: 8, z: 8, core: 2. Of those that a mesh axis runs over, the one named last changes fastest.
Arguments:
- volts: bfloat16 [2, 1024, 32, 14336], P(None, ('inp', 'chan')), may hold values from -6 to 6
- pfb_taps: float32 [6, 2048], replicated, may hold values from -2.5 to 2.5
- channel_order: int32 [32], replicated, may hold values from 0 to 31, each once
- station_slot: int32 [512], replicated, may hold values from 0 to 511, each once
Outputs:
- visibilities: float32 [32, 2, 2, 1024, 1024], P('chan', None, None, 'inp')
Inputs may be any that keep to these rules, and one draw needn't show every extreme that they name: `channel_order`: each coarse channel appears once. `station_slot`: each input pair carries one station.
All inputs are finite; a program needn't handle non-finite values.
Results may differ from a plain program's by a relative error of at most 0.0053.
Values may be sent and summed in bfloat16 or wider, within the bound.
A program may use at most 64 MiB of HBM per device.

v0:
```python
import math

import jax
import jax.numpy as jnp
from jax import lax
from jax.sharding import PartitionSpec as P

FA = 64
FGROUP = 1024


def dft_table(length):
    index = jnp.arange(length, dtype=jnp.int32)
    product = index[:, None] * index[None, :] % length
    angle = product.astype(jnp.float32) * (2.0 * math.pi / length)
    factor = 1.0 / math.sqrt(length)
    cosine = jnp.cos(angle) * factor
    sine = jnp.sin(angle) * factor
    upper = jnp.concatenate([cosine, -sine], 1)
    lower = jnp.concatenate([sine, cosine], 1)
    return jnp.concatenate([upper, lower], 0).astype(jnp.bfloat16)


def twiddle(first, second):
    total = first * second
    inner = jnp.arange(second, dtype=jnp.int32)
    outer = jnp.arange(first, dtype=jnp.int32)
    product = inner[:, None] * outer[None, :] % total
    angle = product.astype(jnp.float32) * (2.0 * math.pi / total)
    return (jnp.cos(angle), jnp.sin(angle))


def transform(stacked, first):
    rows = stacked.shape[0]
    fine = stacked.shape[1] // 2
    second = fine // first
    shaped = stacked.reshape(rows, 2, first, second)
    shaped = jnp.transpose(shaped, (0, 3, 1, 2)).reshape(rows, second, 2 * first)
    sectioned = jnp.einsum(
        "rbk,kq->rbq", shaped, dft_table(first), preferred_element_type=jnp.float32
    )
    real_part = sectioned[:, :, :first]
    imag_part = sectioned[:, :, first:]
    cosine, sine = twiddle(first, second)
    turned_re = real_part * cosine + imag_part * sine
    turned_im = imag_part * cosine - real_part * sine
    section = jnp.stack([turned_re, turned_im], 2).astype(jnp.bfloat16)
    section = jnp.transpose(section, (0, 3, 2, 1)).reshape(rows, first, 2 * second)
    result = jnp.einsum(
        "rak,kq->raq", section, dft_table(second), preferred_element_type=jnp.float32
    )
    result = result.reshape(rows, first, 2, second)
    result = jnp.transpose(result, (0, 2, 3, 1)).reshape(rows, 2 * fine)
    return result.astype(jnp.bfloat16)


def filterbank(volts, pfb_taps):
    two, count, chans, samples = volts.shape
    ntaps, fine = pfb_taps.shape
    frames_all = samples // fine
    spec = frames_all - ntaps + 1
    frames = volts.reshape(two, count, chans, frames_all, fine)
    filtered = jnp.zeros((two, count, chans, spec, fine), jnp.float32)
    for tap in range(ntaps):
        filtered = filtered + pfb_taps[tap] * frames[:, :, :, tap : tap + spec, :].astype(
            jnp.float32
        )
    filtered = filtered.astype(jnp.bfloat16)
    stacked = jnp.moveaxis(filtered, 0, 3).reshape(count * chans * spec, 2 * fine)
    spectra = transform(stacked, FA)
    return spectra.reshape(count, chans, spec, 2 * fine)


def cross_operands(spectra, group):
    count, chans, spec, width = spectra.shape
    fine = width // 2
    groups = fine // group
    parts = spectra.reshape(count, chans, spec, 2, groups, group)
    parts = jnp.transpose(parts, (3, 1, 4, 0, 2, 5)).reshape(2, chans, groups, count, spec * group)
    real_part = parts[0]
    imag_part = parts[1]
    right = jnp.concatenate([real_part, imag_part], -1)
    left = jnp.concatenate([right, jnp.concatenate([imag_part, -real_part], -1)], 2)
    return (left, right)


def correlate(left, piece):
    scale = 1.0 / (left.shape[-1] // 2)
    return jnp.einsum("cgak,cgbk->cgab", left, piece, preferred_element_type=jnp.float32) * scale


def local(volts, pfb_taps, channel_order, station_slot):
    inverse = jnp.argsort(channel_order)
    ordered = jnp.take(volts, inverse, axis=2)
    turned = lax.all_to_all(ordered, "chan", split_axis=2, concat_axis=1, tiled=True)
    spectra = filterbank(turned, pfb_taps)
    left, right = cross_operands(spectra, FGROUP)
    chans, groups, count, depth = right.shape
    inputs = 2 * station_slot.shape[0]
    position = jnp.arange(inputs, dtype=jnp.int32)
    columns = 2 * jnp.take(station_slot, position // 2) + position % 2
    full = correlate(left, lax.all_gather(right, "inp", axis=2, tiled=True))
    vis = full.reshape(chans, groups, 2, count, inputs)
    return jnp.take(vis, columns, axis=4)


def solution(mesh):
    in_specs = (P(None, ("inp", "chan"), None, None), P(), P(), P())
    out_specs = P("chan", None, None, "inp", None)
    return jax.shard_map(local, mesh=mesh, in_specs=in_specs, out_specs=out_specs, check_vma=False)
```

profile of v0, /device:TPU:1, one launch (start us, length us, event | category | flops | bytes accessed | tf_op | source)
XLA Modules:
  0.0 457.4 jit_solution(3648417700805498901)
XLA Ops:
  6.5 0.0 copy-start
  6.5 2.3 sort.17
  8.8 0.0 copy-done
  8.9 6.9 %gather_fusion = s32[1024]{0:T(1024)S(1)} fusion(s32[512]{0:T(512)S(1)} %copy-done, s32[1024]{0:T(1024)S(1)} %broadcast_clamp_fusion.1), kind=kCustom, calls=%fused_computation | custom fusion | bytes 12288 | tf_op jit(solution)/shard_map/jit(_take)/gather | solution.py:101
  15.8 11.0 %gather_fusion.1 = bf16[32,2,2,14336]{3,0,2,1:T(8,128)(2,1)} fusion(bf16[2,2,32,14336]{3,2,1,0:T(8,128)(2,1)} %param.4, s32[1024]{0:T(1024)S(1)} %get-tuple-element.27), kind=kCustom, calls=%fused_computation.1 | custom fusion | bytes 7340160 | tf_op jit(solution)/shard_map/jit(_take)/gather | solution.py:94
  26.8 2.5 select_bitcast_fusion
  29.2 5.6 %copy.27 = bf16[2,2,32,14336]{3,1,0,2:T(2,128)(2,1)} copy(bf16[2,2,32,14336]{3,2,1,0:T(8,128)(2,1)S(1)} %select_bitcast_fusion) | data formatting | bytes 7340032 | tf_op jit(solution)/shard_map/jit(_take)/select_n | solution.py:94
  34.8 0.0 copy-start.4
  34.8 11.4 %all-to-all-start = ((bf16[2,2,32,14336]{3,1,0,2:T(2,128)(2,1)}), bf16[2,2,32,14336]{3,1,0,2:T(2,128)(2,1)}, u32[]{:S(2)}, u32[]{:S(2)}) async-start(bf16[2,2,32,14336]{3,1,0,2:T(2,128)(2,1)} %copy.27), calls=%async_computation | async-start | bytes 7340032 | tf_op jit(solution)/shard_map/all_to_all | solution.py:95
  46.3 0.4 all-gather.2.cloned.1.call-start
  46.7 0.1 fusion.40
  46.7 0.1 fusion.27
  46.9 0.1 negate_convert_fusion.1
  47.0 0.1 maximum_maximum_fusion
  47.1 0.1 fusion.41
  47.2 0.2 negate_convert_fusion
  47.3 0.0 copy-done.4
  47.4 82.5 %all-to-all-done = bf16[2,2,32,14336]{3,1,0,2:T(2,128)(2,1)} async-done(((bf16[2,2,32,14336]{3,1,0,2:T(2,128)(2,1)}), bf16[2,2,32,14336]{3,1,0,2:T(2,128)(2,1)}, u32[]{:S(2)}, u32[]{:S(2)}) %all-to-all-start) | async-done | bytes 3670048 | tf_op jit(solution)/shard_map/all_to_all | solution.py:95
  129.8 6.4 %copy.28 = bf16[2,32,2,1,14336]{4,2,1,0,3:T(2,128)(2,1)} copy(bf16[2,32,2,1,14336]{4,2,0,1,3:T(2,128)(2,1)} %bitcast.4) | data formatting | bytes 7340032 | tf_op jit(solution)/shard_map/all_to_all | solution.py:95
  136.2 9.5 %reshape.221 = bf16[2,64,1,7,2048]{4,3,1,0,2:T(8,128)(2,1)} reshape(bf16[2,32,2,1,14336]{4,2,1,0,3:T(2,128)(2,1)} %copy.28) | data formatting | bytes 7340032 | tf_op jit(solution)/shard_map/reshape | solution.py:62
  145.7 15.9 %fusion.57 = (bf16[2,64,1,2,2048]{4,3,1,0,2:T(2,128)(2,1)S(1)}, bf16[2,64,1,2,2048]{4,3,1,0,2:T(2,128)(2,1)S(1)}, bf16[2,64,1,2,2048]{4,3,1,0,2:T(2,128)(2,1)S(1...) fusion(bf16[2,64,1,7,2048]{4,3,1,0,2:T(8,128)(2,1)} %reshape.221), kind=kLoop, calls=%fused_computation.105 | loop fusion | bytes 12582912 | tf_op jit(solution)/shard_map/slice | solution.py:65
  161.7 3.3 fusion.11
  165.0 1.1 copy.35
  166.1 3.5 reshape_reshape.4
  169.6 6.9 %copy.44 = bf16[128,32,128]{0,2,1:T(8,128)(2,1)S(1)} copy(bf16[128,32,128]{1,2,0:T(8,128)(2,1)} %bitcast.62) | data formatting | bytes 2097152 | tf_op jit(solution)/shard_map/reshape | solution.py:38
  176.6 0.5 fusion.17
  177.0 0.9 fusion.12
  177.9 0.1 pad_maximum_fusion
  178.0 0.9 fusion.6
  179.0 3.5 copy.39
  182.5 1.3 convert_element_type.86
  183.7 0.7 fusion.58
  184.5 0.4 copy.41
  184.9 0.4 squeeze.7
  185.3 0.4 copy.40
  185.7 0.4 squeeze.6
  186.1 0.9 fusion.59
  187.1 0.0 copy-start.2
  187.1 1.0 copy-done.2
  188.0 0.0 all-gather.2.cloned.1.call-update
  188.1 232.4 %all-gather.2.cloned.1.call-done = bf16[1,2,1024,4096]{3,2,1,0:T(8,128)(2,1)} async-done(((bf16[1,2,64,4096]{3,2,1,0:T(8,128)(2,1)}), bf16[1,2,1024,4096]{3,2,1,0:T(8,128)(2,1)}) %all-gather.2.cloned.1.call-update) | async-done | bytes 16777232 | tf_op jit(solution)/shard_map/all_gather | solution.py:102
  420.5 0.0 copy-done.3
  420.5 11.8 %fusion.7 = f32[2,128,1024]{2,1,0:T(8,128)S(1)} fusion(bf16[1,2,1024,4096]{3,2,1,0:T(8,128)(2,1)} %all-gather.2.cloned.1.call-done, bf16[1,2,64,2048]{3,2,1,0:T(8,128)(2,1)S(1)} %copy-done.3, bf16[1,2,64,2048]{3,2,1,0:T(8,128)(2,1)S(1)} %squeeze.7, bf16[1,2,64,4096]{3,2,1,0:T(8,128)(2,1)} %copy-done.2), kind=kOutput, calls=%fused_computation.15 | convolution fusion | flops 2154037248 | bytes 19922944 | tf_op jit(solution)/shard_map/cgak,cgbk->cgab/dot_general | solution.py:89
  432.3 1.1 copy.42
  433.4 9.2 %gather_fusion.2 = f32[1024,2,2,64]{3,2,1,0:T(2,128)} fusion(f32[2,2,64,1024]{2,1,3,0:T(2,128)S(1)} %copy.42, s32[1024]{0:T(1024)S(1)} %get-tuple-element.28), kind=kCustom, calls=%fused_computation.2 | custom fusion | bytes 2101248 | tf_op jit(solution)/shard_map/jit(_take)/gather | solution.py:104
  442.6 5.2 %bitcast_select_fusion = f32[1,2,2,64,1024]{3,2,1,4,0:T(2,128)S(1)} fusion(f32[1024,2,2,64]{3,2,1,0:T(2,128)} %gather_fusion.2, pred[1024]{0:T(1024)(128)(4,1)S(1)} %compare_and_fusion), kind=kLoop, calls=%fused_computation.11 | loop fusion | flops 262144 | bytes 2098176 | tf_op jit(solution)/shard_map/jit(_take)/select_n | solution.py:104
  447.8 2.5 copy.43
  450.4 0.0 copy-done.1
  (12 shorter events, 0.1 us)
Async XLA Ops:
  6.5 2.3 copy-start
  34.8 12.5 %copy-start.4 = (f32[6,2048]{1,0:T(8,128)S(1)}, f32[6,2048]{1,0:T(8,128)}, u32[]{:S(2)}) copy-start(f32[6,2048]{1,0:T(8,128)} %param.5) | copy-start | bytes 147460
  34.8 95.0 %all-to-all-start = ((bf16[2,2,32,14336]{3,1,0,2:T(2,128)(2,1)}), bf16[2,2,32,14336]{3,1,0,2:T(2,128)(2,1)}, u32[]{:S(2)}, u32[]{:S(2)}) async-start(bf16[2,2,32,14336]{3,1,0,2:T(2,128)(2,1)} %copy.27), calls=%async_computation | async-start | bytes 7340032 | tf_op jit(solution)/shard_map/all_to_all | solution.py:95
  46.3 374.2 %all-gather.2.cloned.1.call-start = ((), (), s32[]{:S(2)}) async-start(), calls=%async_computation.1 | async-start | bytes 17825792 | tf_op jit(solution)/shard_map/all_gather | solution.py:102
  187.0 233.5 %copy-start.3 = (bf16[1,2,64,2048]{3,2,1,0:T(8,128)(2,1)S(1)}, bf16[1,2,64,2048]{3,2,1,0:T(8,128)(2,1)}, u32[]{:S(2)}) copy-start(bf16[1,2,64,2048]{3,2,1,0:T(8,128)(2,1)} %get-tuple-element.17) | copy-start | bytes 1572868
  187.1 1.0 copy-start.2
  442.6 7.8 %copy-start.1 = (s32[512]{0:T(512)S(1)}, s32[512]{0:T(512)}, u32[]{:S(2)}) copy-start(s32[512]{0:T(512)} %param.7) | copy-start | bytes 6148
Sparse Core Ops, SparseCore 0:
  188.2 232.2 all-gather.1
where the time goes:
time: 466 us; the launch traced here: 457 us
  waiting for transfers between devices  315 us (68%)
  local copies, waits for them, and re-layouts  87.8 us (19%)
  other arithmetic  15.9 us (3%)
  between operations  13.8 us (3%)
  matrix products  13.2 us (3%)
  starting transfers between devices  11.8 us (3%)
    all_gather x1, waiting for transfers between devices, local(): full = correlate(left, lax.all_gather(right, 'inp', axis=2, tiled=True))  232 us
    all_to_all x1, waiting for transfers between devices, local(): lax.all_to_all(ordered, 'chan', split_axis=2, concat_axis=1, tiled=True)  82.5 us
    slice x1, local copies, waits for them, and re-layouts, filterbank(): frames[:, :, :, tap:tap + spec, :].astype(jnp.float32)  15.9 us
    dot_general x1, matrix products, correlate(): jnp.einsum('cgak,cgbk->cgab', left, piece, preferred_element_type=jnp.flo...  11.8 us
    all_to_all x1, starting transfers between devices, local(): lax.all_to_all(ordered, 'chan', split_axis=2, concat_axis=1, tiled=True)  11.4 us
    gather x1, local copies, waits for them, and re-layouts, local(): ordered = jnp.take(volts, inverse, axis=2)  11 us
    reshape x1, local copies, waits for them, and re-layouts, filterbank(): frames = volts.reshape(two, count, chans, frames_all, fine)  9.54 us
  transfers between devices with their start and end apart: 2, of which 2 were waited for; matrix products, arithmetic and copies ran while one was open for 0% of the time, Pallas kernels for 0%

commit v1 on v0

v1 whole, which is shorter than its diff:
```python
import functools
import math

import jax
import jax.numpy as jnp
import numpy as np
from jax import lax
from jax.experimental import pallas as pl
from jax.experimental.pallas import tpu as pltpu
from jax.sharding import PartitionSpec as P

F32 = jnp.float32
BF16 = jnp.bfloat16
MESH = pl.DeviceIdType.MESH

TAPS = 6
FINE = 2048
N1 = 16
N2 = 128
CH = 32
Z = 8
PLANE = 2 * CH
HALF = 8
FAR = 4
PARTS = 8
SCALE = 2.0**-22


def tables():
    j2 = np.arange(N2)
    f1 = np.arange(N1)
    angle = 2 * math.pi * (f1[:, None] * j2[None, :]) / FINE
    twiddle = np.stack([np.cos(angle), np.sin(angle)]).astype(np.float32)
    theta = 2 * math.pi * (j2[:, None] * j2[None, :] % N2) / N2
    cosine, sine = np.cos(theta), np.sin(theta)
    full = np.zeros((2, N2, 2, 2, 64))
    for g in range(2):
        part = slice(64 * g, 64 * g + 64)
        full[0, :, g, 0] = cosine[:, part]
        full[1, :, g, 0] = sine[:, part]
        full[0, :, g, 1] = -sine[:, part]
        full[1, :, g, 1] = cosine[:, part]
    dft = full.reshape(256, 256).astype(jnp.bfloat16)
    shuffle = np.zeros((256, 256))
    for slot in range(16):
        for a in range(2):
            for f in range(HALF):
                shuffle[f * 32 + slot * 2 + a, slot * 16 + a * 8 + f] = 1
    turn = np.zeros((256, 256))
    for s in range(2):
        for f in range(64):
            turn[s * 128 + 64 + f, s * 128 + f] = 1
            turn[s * 128 + f, s * 128 + 64 + f] = -1
    return twiddle, dft, shuffle.astype(jnp.bfloat16), turn.astype(jnp.bfloat16)


def dft4(v):
    (ar, ai), (br, bi), (cr, ci), (dr, di) = v
    pr, pi, mr, mi = ar + cr, ai + ci, ar - cr, ai - ci
    qr, qi, nr, ni = br + dr, bi + di, br - dr, bi - di
    return [
        (pr + qr, pi + qi),
        (mr + ni, mi - nr),
        (pr - qr, pi - qi),
        (mr - ni, mi + nr),
    ]


def rotate(v, k):
    k = k % 16
    re, im = v
    if k == 0:
        return v
    if k == 4:
        return im, -re
    c, s = math.cos(2 * math.pi * k / 16), math.sin(2 * math.pi * k / 16)
    if k == 2:
        return (re + im) * c, (im - re) * c
    if k == 6:
        return (im - re) * s, (re + im) * -s
    return re * c + im * s, im * c - re * s


def dft16(x):
    inner = [dft4([x[4 * n + m] for n in range(4)]) for m in range(4)]
    out = [None] * 16
    for k in range(4):
        column = dft4([rotate(inner[m][k], m * k) for m in range(4)])
        for q in range(4):
            out[k + 4 * q] = column[q]
    return out


def spectra_kernel(volts, taps, order, twiddle, dft, out, section, mover, first):
    a = pl.program_id(0)

    @pl.when(a == 0)
    def _():
        spread = lax.broadcasted_iota(jnp.int32, (CH, 512), 1) % CH
        spread = spread == lax.broadcasted_iota(jnp.int32, (CH, 512), 0)
        rows = jnp.broadcast_to(order[...], (8, CH)).astype(F32).astype(BF16)
        goal = jnp.dot(rows, spread.astype(F32).astype(BF16), preferred_element_type=F32)[0:1]
        row = lax.broadcasted_iota(jnp.int32, (512, 512), 0)
        col = lax.broadcasted_iota(jnp.int32, (512, 512), 1)
        same = (row // N1 == goal.astype(jnp.int32)) & (row % N1 == col // CH)
        mover[...] = same.astype(F32).astype(BF16)

    for s in range(2):
        for h in range(2):
            rows = pl.ds(h * 16, 16)

            def point(p, j):
                total = None
                for t in range(TAPS):
                    at = (s + t) * FINE + j * N2
                    term = taps[t : t + 1, j * N2 : (j + 1) * N2] * volts[
                        p, 0, rows, at : at + N2
                    ].astype(F32)
                    total = term if total is None else total + term
                return total.astype(BF16).astype(F32)

            x = [(point(0, j), point(1, j)) for j in range(N1)]
            for f, (re, im) in enumerate(dft16(x)):
                c, d = twiddle[0, f : f + 1], twiddle[1, f : f + 1]
                at = pl.ds(f * CH + h * 16, 16)
                section[at, 0:N2] = (re * c + im * d).astype(BF16)
                section[at, N2 : 2 * N2] = (im * c - re * d).astype(BF16)
        moved = jnp.dot(mover[...], section[...], preferred_element_type=F32).astype(BF16)
        result = jnp.dot(moved, dft[...], preferred_element_type=F32)
        result = result.reshape(CH, 2, HALF, 256)

        @pl.when(a == 0)
        def _():
            first[s] = result

        @pl.when(a == 1)
        def _():
            other = first[s]
            for h in range(2):
                both = jnp.concatenate([other[:, h], result[:, h]], axis=1).astype(BF16)
                for g in range(2):
                    out[h, g, :, :, s * 128 : (s + 1) * 128] = both[:, :, g * 128 : (g + 1) * 128]


def spectra(volts, taps, order, twiddle, dft):
    samples = volts.shape[-1]
    return pl.pallas_call(
        spectra_kernel,
        grid=(2,),
        out_shape=jax.ShapeDtypeStruct((2, 2, CH, 16, 256), BF16),
        in_specs=[
            pl.BlockSpec((2, 1, CH, samples), lambda a: (0, a, 0, 0)),
            pl.BlockSpec((TAPS, FINE), lambda a: (0, 0)),
            pl.BlockSpec((1, CH), lambda a: (0, 0)),
            pl.BlockSpec((2, N1, N2), lambda a: (0, 0, 0)),
            pl.BlockSpec((256, 256), lambda a: (0, 0)),
        ],
        out_specs=pl.BlockSpec((2, 2, CH, 16, 256), lambda a: (0, 0, 0, 0, 0)),
        scratch_shapes=[
            pltpu.VMEM((512, 256), BF16),
            pltpu.VMEM((512, 512), BF16),
            pltpu.VMEM((2, CH, 2, HALF, 256), F32),
        ],
        compiler_params=pltpu.CompilerParams(vmem_limit_bytes=40 * 2**20),
        name="spectra",
    )(volts, taps, order, twiddle, dft)


def cross_kernel(
    sent, slots, shuffle, turn, out,
    arrived, blocks, left, total, places, final, partner, mirror,
    own_sem, turn_send, turn_recv, ring_send, ring_recv,
    final_recv, partner_send, mirror_send,
):
    chan = lax.axis_index("chan")
    inp = lax.axis_index("inp")
    g = inp // Z
    z = inp % Z
    me = g * CH + chan
    way = 1 - 2 * (chan % 2)

    def along(hops):
        return (z + hops * way + Z) % Z

    def in_plane(k):
        peer = (me + k) % PLANE
        return peer, (peer % CH, (peer // CH) * Z + z)

    barrier = pltpu.get_barrier_semaphore()

    def greet_plane(k, _):
        pl.semaphore_signal(barrier, inc=1, device_id=in_plane(k)[1], device_id_type=MESH)
        return 0

    def greet_column(k, _):
        there = (z + k) % Z
        for x in range(2):
            pl.semaphore_signal(
                barrier, inc=1, device_id=(chan, x * Z + there), device_id_type=MESH
            )
        return 0

    lax.fori_loop(1, PLANE, greet_plane, 0)
    lax.fori_loop(1, Z, greet_column, 0)
    pl.semaphore_wait(barrier, PLANE - 1 + 2 * (Z - 1))

    for h in range(2):
        pltpu.make_async_copy(sent.at[h, me], arrived.at[h, me], own_sem.at[h]).start()

        def send(k, _):
            peer, device = in_plane(k)
            pltpu.make_async_remote_copy(
                src_ref=sent.at[h, peer],
                dst_ref=arrived.at[h, me],
                send_sem=turn_send.at[h],
                recv_sem=turn_recv.at[h],
                device_id=device,
                device_id_type=MESH,
            ).start()
            return 0

        lax.fori_loop(1, PLANE, send, 0)

    def one_hot(e, _):
        value = jnp.broadcast_to(slots[...], (8, 512))
        spread = lax.broadcasted_iota(jnp.int32, (512, 1024), 1) // 2
        spread = spread == lax.broadcasted_iota(jnp.int32, (512, 1024), 0)
        spread = spread.astype(F32).astype(BF16)
        high = jnp.dot((value // 32).astype(F32).astype(BF16), spread, preferred_element_type=F32)
        low = jnp.dot((value % 32).astype(F32).astype(BF16), spread, preferred_element_type=F32)
        station = (high * 32.0 + low)[0:1].astype(jnp.int32)
        source = 2 * station + lax.broadcasted_iota(jnp.int32, (1, 1024), 1) % 2
        row = lax.broadcasted_iota(jnp.int32, (128, 1), 0)
        row = (row // 64) * (64 * Z) + row % 64 + along(-e) * 64
        places[e] = (source == row).astype(F32).astype(BF16)
        return 0

    lax.fori_loop(0, 8, one_hot, 0)

    def piece(ref, d, q):
        return ref.at[d, pl.ds(q * 2, 2)]

    def pass_on(d, q):
        return pltpu.make_async_remote_copy(
            src_ref=piece(blocks, d, q),
            dst_ref=piece(blocks, d + 1, q),
            send_sem=ring_send.at[d, q],
            recv_sem=ring_recv.at[d, q],
            device_id=(chan, g * Z + along(1)),
            device_id_type=MESH,
        )

    def multiply(d, f):
        total[...] += lax.dot_general(
            left[f], blocks[d, f], (((1,), (1,)), ((), ())), preferred_element_type=F32
        )

    def to_partner(d):
        return pltpu.make_async_remote_copy(
            src_ref=partner.at[d],
            dst_ref=final.at[d, g],
            send_sem=partner_send.at[d],
            recv_sem=final_recv.at[d, g],
            device_id=(chan, (1 - g) * Z + z),
            device_id_type=MESH,
        )

    def to_column(d, x):
        return pltpu.make_async_remote_copy(
            src_ref=mirror.at[d, x],
            dst_ref=final.at[8 - d, g],
            send_sem=mirror_send.at[d, x],
            recv_sem=final_recv.at[8 - d, g],
            device_id=(chan, x * Z + along(-d)),
            device_id_type=MESH,
        )

    def finish(d):
        for p in range(2):
            mine = pl.ds(pl.multiple_of(p * 128 + g * 64, 64), 64)
            other = pl.ds(pl.multiple_of(p * 128 + (1 - g) * 64, 64), 64)
            final[d, g, p] = total[mine, :].astype(BF16)
            partner[d, p] = total[other, :].astype(BF16)
        to_partner(d).start()

    for h in range(2):
        pltpu.make_async_copy(sent.at[h, me], arrived.at[h, me], own_sem.at[h]).wait()
        several = arrived.at[h, pl.ds(0, PLANE - 1)]
        pltpu.make_async_copy(several, several, turn_recv.at[h]).wait()

        def arrange(q, _):
            rows = arrived[h, pl.ds(q * 16, 16)].reshape(256, 256)
            rows = jnp.dot(shuffle[...], rows, preferred_element_type=F32).astype(BF16)
            turned = jnp.dot(rows, turn[...], preferred_element_type=F32).astype(BF16)
            at = pl.ds(pl.multiple_of(q * 32, 32), 32)
            low = pl.ds(pl.multiple_of(q * 32 + 128, 32), 32)
            several = pl.ds(h * HALF, HALF)
            blocks[0, several, at, :] = rows.reshape(HALF, 32, 256)
            left[several, at, :] = rows.reshape(HALF, 32, 256)
            left[several, low, :] = turned.reshape(HALF, 32, 256)
            return 0

        lax.fori_loop(0, PLANE // 16, arrange, 0)

        def start(q, _):
            pass_on(0, q).start()
            return 0

        lax.fori_loop(h * PARTS // 2, (h + 1) * PARTS // 2, start, 0)

    total[...] = jnp.zeros_like(total)

    def own(f, _):
        multiply(0, f)
        return 0

    lax.fori_loop(0, N1, own, 0)
    finish(0)

    def hop(d, _):
        total[...] = jnp.zeros_like(total)

        def step(q, _):
            pass_on(d - 1, q).wait_recv()

            @pl.when(d < FAR)
            def _():
                pass_on(d, q).start()

            multiply(d, 2 * q)
            multiply(d, 2 * q + 1)
            return 0

        lax.fori_loop(0, PARTS, step, 0)
        finish(d)

        @pl.when(d < FAR)
        def _():
            re = total[0:128, :].T
            im = -total[128:256, :].T
            for x in range(2):
                mirror[d, x, 0] = re[x * 64 : (x + 1) * 64].astype(BF16)
                mirror[d, x, 1] = im[x * 64 : (x + 1) * 64].astype(BF16)
                to_column(d, x).start()

        return 0

    lax.fori_loop(1, FAR + 1, hop, 0)

    def from_partner(d, _):
        there = final.at[d, 1 - g]
        pltpu.make_async_copy(there, there, final_recv.at[d, 1 - g]).wait()
        return 0

    lax.fori_loop(0, FAR + 1, from_partner, 0)

    def from_column(d, _):
        for x in range(2):
            there = final.at[8 - d, x]
            pltpu.make_async_copy(there, there, final_recv.at[8 - d, x]).wait()
        return 0

    lax.fori_loop(1, FAR, from_column, 0)

    for n in range(4):
        columns = slice(n * 256, (n + 1) * 256)
        tile = jnp.zeros((256, 256), F32)
        for e in range(8):
            tile += jnp.dot(
                final[e].reshape(256, 128), places[e, :, columns], preferred_element_type=F32
            )
        out[0, :, :, :, columns] = (tile * SCALE).reshape(2, 2, 64, 256)

    for h in range(2):
        several = sent.at[h, pl.ds(0, PLANE - 1)]
        pltpu.make_async_copy(several, several, turn_send.at[h]).wait()

    def drain(d, _):
        to_partner(d).wait_send()

        @pl.when(d < FAR)
        def _():
            def one(q, _):
                pass_on(d, q).wait_send()
                return 0

            lax.fori_loop(0, PARTS, one, 0)

            @pl.when(d > 0)
            def _():
                for x in range(2):
                    to_column(d, x).wait_send()

        return 0

    lax.fori_loop(0, FAR + 1, drain, 0)


def cross(sent, slots, shuffle, turn):
    dma = pltpu.SemaphoreType.DMA
    return pl.pallas_call(
        cross_kernel,
        out_shape=jax.ShapeDtypeStruct((1, 2, 2, 64, 1024), F32),
        in_specs=[pl.BlockSpec(memory_space=pl.ANY)] + [pl.BlockSpec(memory_space=pltpu.VMEM)] * 3,
        out_specs=pl.BlockSpec(memory_space=pltpu.VMEM),
        scratch_shapes=[
            pltpu.VMEM((2, PLANE, 16, 256), BF16),
            pltpu.VMEM((FAR + 1, N1, 128, 256), BF16),
            pltpu.VMEM((N1, 256, 256), BF16),
            pltpu.VMEM((256, 128), F32),
            pltpu.VMEM((8, 128, 1024), BF16),
            pltpu.VMEM((8, 2, 2, 64, 128), BF16),
            pltpu.VMEM((FAR + 1, 2, 64, 128), BF16),
            pltpu.VMEM((FAR, 2, 2, 64, 128), BF16),
            dma((2,)),
            dma((2,)),
            dma((2,)),
            dma((FAR, PARTS)),
            dma((FAR, PARTS)),
            dma((8, 2)),
            dma((FAR + 1,)),
            dma((FAR, 2)),
        ],
        compiler_params=pltpu.CompilerParams(
            collective_id=0, has_side_effects=True, vmem_limit_bytes=40 * 2**20
        ),
        name="cross",
    )(sent, slots, shuffle, turn)


def local(volts, pfb_taps, channel_order, station_slot):
    twiddle, dft, shuffle, turn = tables()
    result = spectra(volts, pfb_taps, channel_order.reshape(1, CH), twiddle, dft)
    sent = result.reshape(2, PLANE, 16, 256)
    return cross(sent, station_slot.reshape(1, -1), shuffle, turn)


def solution(mesh):
    in_specs = (P(None, ("inp", "chan"), None, None), P(), P(), P())
    out_specs = P("chan", None, None, "inp", None)
    return jax.shard_map(local, mesh=mesh, in_specs=in_specs, out_specs=out_specs, check_vma=False)
```

time: 466 us -> 106 us (0.23)
  the two profiles are of different devices: /device:TPU:1 before, /device:TPU:6 now
where the time goes in v1:
time: 106 us; the launch traced here: 105 us
  Pallas kernels  99.1 us (93%)
  local copies, waits for them, and re-layouts  6.15 us (6%)
    pallas_call x1, Pallas kernels, cross(): pl.pallas_call(cross_kernel, out_shape=jax.ShapeDtypeStruct((1, 2, 2, 64,...  94.3 us
    unnamed x17, local copies, waits for them, and re-layouts  6.15 us
    pallas_call x1, Pallas kernels, spectra(): pl.pallas_call(spectra_kernel, grid=(2,), out_shape=jax.ShapeDtypeStruct(...  4.78 us

profile of v1, /device:TPU:6, one launch (start us, length us, event | category | flops | bytes accessed | tf_op | source)
XLA Modules:
  0.0 105.3 jit_solution(7325867363768687113)
XLA Ops:
  0.0 0.0 copy-start.6
  0.0 0.0 copy-start
  0.0 2.0 %copy-done = bf16[2,2,32,14336]{3,2,1,0:T(8,128)(2,1)S(1)} copy-done((bf16[2,2,32,14336]{3,2,1,0:T(8,128)(2,1)S(1)}, bf16[2,2,32,14336]{3,2,1,0:T(8,128)(2,1)}, u32[]{:S(2)}) %copy-start) | copy-done | bytes 3670040
  2.1 0.0 copy-start.1
  2.1 0.9 copy-done.1
  3.0 0.0 copy-start.4
  3.0 0.8 copy-done.4
  3.8 0.0 copy-start.5
  3.8 0.7 copy-done.5
  4.5 0.0 copy-start.7
  4.5 0.7 copy-done.7
  5.2 0.0 copy-start.2
  5.2 0.0 copy-start.3
  5.2 4.8 %spectra.1 = bf16[2,2,32,16,256]{4,3,2,1,0:T(8,128)(2,1)S(1)} custom-call(bf16[2,2,32,14336]{3,2,1,0:T(8,128)(2,1)S(1)} %copy-done, f32[6,2048]{1,0:T(8,128)S(1)} %copy-done.4, s32[1,32]{1,0:T(1,128)S(1)} %bitcast.5, f32[2,16,128]{2,1,0:T(8,128)S(1)} %copy-done.5, bf16[256,256]{1,0:T(8,128)(2,1)S(1)} %copy-done.1), custom_call_target="tpu_custom_call" | custom-call | tf_op jit(solution)/shard_map/spectra/pallas_call | solution.py:147
  10.0 0.0 copy-done.6
  10.0 0.0 copy-done.2
  10.0 0.0 copy-done.3
  10.0 94.3 %cross.1 = f32[1,2,2,64,1024]{4,3,2,1,0:T(8,128)S(1)} custom-call(bf16[2,64,16,256]{3,2,1,0:T(8,128)(2,1)S(1)} %bitcast.3, s32[1,512]{1,0:T(1,128)S(1)} %bitcast.4, bf16[256,256]{1,0:T(8,128)(2,1)S(1)} %copy-done.3, bf16[256,256]{1,0:T(8,128)(2,1)S(1)} %copy-done.2), custom_call_target="tpu_custom_call" | custom-call | tf_op jit(solution)/shard_map/cross/pallas_call | solution.py:401
  104.3 1.0 copy.10
Async XLA Ops:
  0.0 10.0 %copy-start.6 = (s32[512]{0:T(512)S(1)}, s32[512]{0:T(512)}, u32[]{:S(2)}) copy-start(s32[512]{0:T(512)} %param.11) | copy-start | bytes 6148
  0.0 2.1 %copy-start = (bf16[2,2,32,14336]{3,2,1,0:T(8,128)(2,1)S(1)}, bf16[2,2,32,14336]{3,2,1,0:T(8,128)(2,1)}, u32[]{:S(2)}) copy-start(bf16[2,2,32,14336]{3,2,1,0:T(8,128)(2,1)} %volts.1) | copy-start | bytes 11010052
  2.1 0.9 copy-start.1
  3.0 0.8 copy-start.4
  3.8 0.7 copy-start.5
  4.5 0.7 copy-start.7
  5.2 4.8 %copy-start.2 = (bf16[256,256]{1,0:T(8,128)(2,1)S(1)}, bf16[256,256]{1,0:T(8,128)(2,1)}, u32[]{:S(2)}) copy-start(bf16[256,256]{1,0:T(8,128)(2,1)} %constant.11.clone.turn) | copy-start | bytes 393220
  5.2 4.8 %copy-start.3 = (bf16[256,256]{1,0:T(8,128)(2,1)S(1)}, bf16[256,256]{1,0:T(8,128)(2,1)}, u32[]{:S(2)}) copy-start(bf16[256,256]{1,0:T(8,128)(2,1)} %constant.10.clone.shuffle) | copy-start | bytes 393220

commit v2 on v1

v2 whole, which is shorter than its diff:
```python
import functools
import math

import jax
import jax.numpy as jnp
import numpy as np
from jax import lax
from jax.experimental import pallas as pl
from jax.experimental.pallas import tpu as pltpu
from jax.sharding import PartitionSpec as P

F32 = jnp.float32
BF16 = jnp.bfloat16
MESH = pl.DeviceIdType.MESH

TAPS = 6
FINE = 2048
N1 = 16
N2 = 128
CH = 32
Z = 8
PLANE = 2 * CH
HALF = 8
QUARTERS = 4
DEEP = 4
FAR = 4
PIECES = 2
SCALE = 2.0**-22


def tables():
    j2 = np.arange(N2)
    f1 = np.arange(N1)
    angle = 2 * math.pi * (f1[:, None] * j2[None, :]) / FINE
    twiddle = np.stack([np.cos(angle), np.sin(angle)]).astype(np.float32)
    theta = 2 * math.pi * (j2[:, None] * j2[None, :] % N2) / N2
    cosine, sine = np.cos(theta), np.sin(theta)
    full = np.zeros((2, N2, 2, 2, 64))
    for g in range(2):
        part = slice(64 * g, 64 * g + 64)
        full[0, :, g, 0] = cosine[:, part]
        full[1, :, g, 0] = sine[:, part]
        full[0, :, g, 1] = -sine[:, part]
        full[1, :, g, 1] = cosine[:, part]
    dft = full.reshape(256, 256).astype(jnp.bfloat16)
    shuffle = np.zeros((256, 256))
    for slot in range(16):
        for a in range(2):
            for f in range(HALF):
                shuffle[f * 32 + slot * 2 + a, slot * 16 + a * 8 + f] = 1
    turn = np.zeros((256, 256))
    for s in range(2):
        for f in range(64):
            turn[s * 128 + 64 + f, s * 128 + f] = 1
            turn[s * 128 + f, s * 128 + 64 + f] = -1
    return twiddle, dft, shuffle.astype(jnp.bfloat16), turn.astype(jnp.bfloat16)


def dft4(v):
    (ar, ai), (br, bi), (cr, ci), (dr, di) = v
    pr, pi, mr, mi = ar + cr, ai + ci, ar - cr, ai - ci
    qr, qi, nr, ni = br + dr, bi + di, br - dr, bi - di
    return [
        (pr + qr, pi + qi),
        (mr + ni, mi - nr),
        (pr - qr, pi - qi),
        (mr - ni, mi + nr),
    ]


def rotate(v, k):
    k = k % 16
    re, im = v
    if k == 0:
        return v
    if k == 4:
        return im, -re
    c, s = math.cos(2 * math.pi * k / 16), math.sin(2 * math.pi * k / 16)
    if k == 2:
        return (re + im) * c, (im - re) * c
    if k == 6:
        return (im - re) * s, (re + im) * -s
    return re * c + im * s, im * c - re * s


def dft16(x):
    inner = [dft4([x[4 * n + m] for n in range(4)]) for m in range(4)]
    out = [None] * 16
    for k in range(4):
        column = dft4([rotate(inner[m][k], m * k) for m in range(4)])
        for q in range(4):
            out[k + 4 * q] = column[q]
    return out


SENDS = 4
LATE = (FAR, FAR + 1)
ORDER = (
    [("send", 1, n) for n in range(SENDS)]
    + [("columns",), ("take", 0)] + [("send", 2, n) for n in range(SENDS)]
    + [("pass", 1, 0), ("take", 1)] + [("send", 3, n) for n in range(SENDS)]
    + [("pass", 2, 0), ("pass", 1, 1), ("pass", 2, 1)]
    + [("take", 2), ("pass", 1, 2), ("take", 3), ("pass", 2, 2), ("pass", 1, 3), ("pass", 2, 3)]
    + [("pass", 3, q) for q in range(QUARTERS)]
    + [("pass", 4, 0), ("pass", 4, 1), ("product",), ("pass", 4, 2), ("pass", 4, 3)]
)


def cross_kernel(
    volts_hbm, taps_hbm, order_hbm, slots_hbm, twiddle_hbm, dft_hbm, shuffle_hbm, turn_hbm, out,
    volts, taps, order, slots, twiddle, dft, shuffle, turn,
    section, mover, first, sent, arrived, blocks, left, total, places, sums, final, partner, mirror,
    volts_sem, small_sem, own_sem, turn_send, turn_recv, ring_send, ring_recv,
    final_recv, partner_send, mirror_send,
):
    chan = lax.axis_index("chan")
    inp = lax.axis_index("inp")
    g = lax.div(inp, Z)
    z = lax.rem(inp, Z)
    me = g * CH + chan
    way = 1 - 2 * lax.rem(chan, 2)

    def along(hops):
        return lax.rem(z + hops * way + Z, Z)

    def peers(act, n=0, parts=1):
        step = CH // 2 // parts
        if n == 0:
            act(1 - g, chan)

        def one(k, _):
            for c in (lax.rem(chan + k, CH), lax.rem(chan + CH - k, CH)):
                act(g, c)
                act(1 - g, c)
            return 0

        lax.fori_loop(max(n * step, 1), (n + 1) * step, one, 0)
        if n == parts - 1:
            far = lax.rem(chan + CH // 2, CH)
            act(g, far)
            act(1 - g, far)

    small = [
        pltpu.make_async_copy(source, target, small_sem.at[n])
        for n, (source, target) in enumerate(
            [
                (order_hbm, order), (taps_hbm, taps), (twiddle_hbm, twiddle), (dft_hbm, dft),
                (slots_hbm, slots), (shuffle_hbm, shuffle), (turn_hbm, turn),
            ]
        )
    ]
    large = [
        [
            pltpu.make_async_copy(volts_hbm.at[p, a], volts.at[a, p], volts_sem.at[a, p])
            for p in range(2)
        ]
        for a in range(2)
    ]
    small[0].start()
    for copy in large[0] + small[1:4] + large[1] + small[4:]:
        copy.start()

    barrier = pltpu.get_barrier_semaphore()

    def greet(x, c):
        pl.semaphore_signal(barrier, inc=1, device_id=(c, x * Z + z), device_id_type=MESH)

    def greet_column(k, _):
        there = lax.rem(z + k, Z)
        for x in range(2):
            pl.semaphore_signal(
                barrier, inc=1, device_id=(chan, x * Z + there), device_id_type=MESH
            )
        return 0

    peers(greet)
    lax.fori_loop(1, Z, greet_column, 0)

    small[0].wait()
    spread = lax.broadcasted_iota(jnp.int32, (CH, 512), 1) % CH
    spread = spread == lax.broadcasted_iota(jnp.int32, (CH, 512), 0)
    rows = jnp.broadcast_to(order[...], (8, CH)).astype(F32).astype(BF16)
    goal = jnp.dot(rows, spread.astype(F32).astype(BF16), preferred_element_type=F32)[0:1]
    row = lax.broadcasted_iota(jnp.int32, (512, 512), 0)
    col = lax.broadcasted_iota(jnp.int32, (512, 512), 1)
    same = (row // N1 == goal.astype(jnp.int32)) & (row % N1 == col // CH)
    mover[...] = same.astype(F32).astype(BF16)

    def transform(s, a):
        for h in range(2):
            rows = pl.ds(h * 16, 16)

            def point(p, j):
                total = None
                for t in range(TAPS):
                    at = (s + t) * FINE + j * N2
                    term = taps[t : t + 1, j * N2 : (j + 1) * N2] * volts[
                        a, p, rows, at : at + N2
                    ].astype(F32)
                    total = term if total is None else total + term
                return total.astype(BF16).astype(F32)

            x = [(point(0, j), point(1, j)) for j in range(N1)]
            for f, (re, im) in enumerate(dft16(x)):
                c, d = twiddle[0, f : f + 1], twiddle[1, f : f + 1]
                at = pl.ds(f * CH + h * 16, 16)
                section[a, at, 0:N2] = (re * c + im * d).astype(BF16)
                section[a, at, N2 : 2 * N2] = (im * c - re * d).astype(BF16)
        moved = jnp.dot(mover[...], section[a], preferred_element_type=F32).astype(BF16)
        result = jnp.dot(moved, dft[...], preferred_element_type=F32)
        return result.reshape(CH, 2, HALF, 256)

    def spectrum(s):
        if s == 0:
            for copy in small[1:4] + large[0]:
                copy.wait()
        first[...] = transform(s, 0)
        if s == 0:
            for copy in large[1]:
                copy.wait()
        second = transform(s, 1)
        for h in range(2):
            both = jnp.concatenate([first[:, h], second[:, h]], axis=1).astype(BF16)
            for k in range(2):
                sent[2 * s + h, k * CH : (k + 1) * CH] = both[:, :, k * 128 : (k + 1) * 128]

    def keep(q):
        return pltpu.make_async_copy(sent.at[q, me], arrived.at[q, me], own_sem.at[q])

    def send(q, n):
        def one(x, c):
            pltpu.make_async_remote_copy(
                src_ref=sent.at[q, x * CH + c],
                dst_ref=arrived.at[q, me],
                send_sem=turn_send.at[q],
                recv_sem=turn_recv.at[q],
                device_id=(c, x * Z + z),
                device_id_type=MESH,
            ).start()

        peers(one, n, SENDS)

    def columns():
        for copy in small[4:]:
            copy.wait()
        value = jnp.broadcast_to(slots[...], (8, 512))
        spread = lax.broadcasted_iota(jnp.int32, (512, 1024), 1) // 2
        spread = spread == lax.broadcasted_iota(jnp.int32, (512, 1024), 0)
        spread = spread.astype(F32).astype(BF16)
        high = jnp.dot((value // 32).astype(F32).astype(BF16), spread, preferred_element_type=F32)
        low = jnp.dot((value % 32).astype(F32).astype(BF16), spread, preferred_element_type=F32)
        station = (high * 32.0 + low)[0:1].astype(jnp.int32)
        source = 2 * station + lax.broadcasted_iota(jnp.int32, (1, 1024), 1) % 2

        def one_hot(e, _):
            row = lax.broadcasted_iota(jnp.int32, (128, 1), 0)
            row = (row // 64) * (64 * Z) + row % 64 + along(-e) * 64
            places[e] = (source == row).astype(F32).astype(BF16)
            return 0

        lax.fori_loop(0, 8, one_hot, 0)

    def pass_on(d, n):
        several = pl.ds(n * (DEEP // PIECES), DEEP // PIECES)
        return pltpu.make_async_remote_copy(
            src_ref=blocks.at[d, several],
            dst_ref=blocks.at[d + 1, several],
            send_sem=ring_send.at[d, n],
            recv_sem=ring_recv.at[d, n],
            device_id=(chan, g * Z + along(1)),
            device_id_type=MESH,
        )

    def multiply(d, start, count):
        value = None
        for k in range(count):
            term = lax.dot_general(
                left[start + k],
                blocks[d, start + k],
                (((1,), (1,)), ((), ())),
                preferred_element_type=F32,
            )
            value = term if value is None else value + term
        total[d] += value

    def take(q):
        keep(q).wait()
        several = arrived.at[q, pl.ds(0, PLANE - 1)]
        pltpu.make_async_copy(several, several, turn_recv.at[q]).wait()

        def arrange(n, _):
            rows = arrived[q, pl.ds(n * 16, 16)].reshape(256, 128)
            rows = jnp.dot(shuffle[...], rows, preferred_element_type=F32)
            rows = rows.reshape(DEEP, 2, 32, 128)
            rows = jnp.concatenate([rows[:, 0], rows[:, 1]], axis=-1).astype(BF16)
            turned = jnp.dot(rows.reshape(DEEP * 32, 256), turn[...], preferred_element_type=F32)
            at = pl.ds(pl.multiple_of(n * 32, 32), 32)
            low = pl.ds(pl.multiple_of(n * 32 + 128, 32), 32)
            several = pl.ds(q * DEEP, DEEP)
            blocks[0, several, at, :] = rows
            left[several, at, :] = rows
            left[several, low, :] = turned.astype(BF16).reshape(DEEP, 32, 256)
            return 0

        lax.fori_loop(0, PLANE // 16, arrange, 0)
        for n in range(PIECES):
            pass_on(0, q * PIECES + n).start()
        multiply(0, q * DEEP, DEEP)

    def receive(d, q):
        def one(n, _):
            pass_on(d - 1, n).wait_recv()
            if d < FAR:
                pass_on(d, n).start()
            multiply(d, n * (DEEP // PIECES), DEEP // PIECES)
            return 0

        lax.fori_loop(q * PIECES, (q + 1) * PIECES, one, 0)

    def to_partner(d):
        return pltpu.make_async_remote_copy(
            src_ref=partner.at[d],
            dst_ref=final.at[d, g],
            send_sem=partner_send.at[d],
            recv_sem=final_recv.at[d, g],
            device_id=(chan, (1 - g) * Z + z),
            device_id_type=MESH,
        )

    def to_column(d, x):
        return pltpu.make_async_remote_copy(
            src_ref=mirror.at[d, x],
            dst_ref=final.at[8 - d, g],
            send_sem=mirror_send.at[d, x],
            recv_sem=final_recv.at[8 - d, g],
            device_id=(chan, x * Z + along(-d)),
            device_id_type=MESH,
        )

    def finish(d):
        for p in range(2):
            mine = pl.ds(pl.multiple_of(p * 128 + g * 64, 64), 64)
            other = pl.ds(pl.multiple_of(p * 128 + (1 - g) * 64, 64), 64)
            final[d, g, p] = total[d, mine, :].astype(BF16)
            partner[d, p] = total[d, other, :].astype(BF16)
        to_partner(d).start()
        if 0 < d < FAR:
            re = total[d, 0:128, :].T
            im = -total[d, 128:256, :].T
            for x in range(2):
                mirror[d, x, 0] = re[x * 64 : (x + 1) * 64].astype(BF16)
                mirror[d, x, 1] = im[x * 64 : (x + 1) * 64].astype(BF16)
                to_column(d, x).start()

    def placed(e, n):
        columns = slice(n * 256, (n + 1) * 256)
        return jnp.dot(
            final[e].reshape(256, 128), places[e, :, columns], preferred_element_type=F32
        )

    def arrives(e, x):
        there = final.at[e, x]
        pltpu.make_async_copy(there, there, final_recv.at[e, x]).wait()

    def product():
        for e in range(8):
            if e < FAR:
                arrives(e, 1 - g)
            if e > FAR + 1:
                arrives(e, 0)
                arrives(e, 1)
        for n in range(4):
            tile = placed(0, n)
            for e in range(1, 8):
                if e not in LATE:
                    tile += placed(e, n)
            sums[n] = tile

    total[...] = jnp.zeros_like(total)
    spectrum(0)
    pl.semaphore_wait(barrier, PLANE - 1 + 2 * (Z - 1))
    for q in (0, 1):
        keep(q).start()
    for n in range(SENDS):
        send(0, n)
    spectrum(1)
    for q in (2, 3):
        keep(q).start()
    for what, *which in ORDER:
        if what == "send":
            send(*which)
        elif what == "take":
            take(*which)
            if which[0] == QUARTERS - 1:
                finish(0)
        elif what == "pass":
            receive(*which)
            if which[1] == QUARTERS - 1:
                finish(which[0])
        elif what == "columns":
            columns()
        else:
            product()
    arrives(FAR + 1, 0)
    arrives(FAR + 1, 1)
    arrives(FAR, 1 - g)
    for n in range(4):
        tile = (sums[n] + placed(FAR + 1, n) + placed(FAR, n)) * SCALE
        out[0, :, :, :, n * 256 : (n + 1) * 256] = tile.reshape(2, 2, 64, 256)

    for q in range(QUARTERS):
        several = sent.at[q, pl.ds(0, PLANE - 1)]
        pltpu.make_async_copy(several, several, turn_send.at[q]).wait()

    def drain(d, _):
        def one(n, _):
            pass_on(d, n).wait_send()
            return 0

        lax.fori_loop(0, QUARTERS * PIECES, one, 0)
        return 0

    lax.fori_loop(0, FAR, drain, 0)
    for d in range(FAR + 1):
        to_partner(d).wait_send()
        if 0 < d < FAR:
            for x in range(2):
                to_column(d, x).wait_send()


def cross(*operands):
    dma = pltpu.SemaphoreType.DMA
    return pl.pallas_call(
        cross_kernel,
        out_shape=jax.ShapeDtypeStruct((1, 2, 2, 64, 1024), F32),
        in_specs=[pl.BlockSpec(memory_space=pl.ANY)] * 8,
        out_specs=pl.BlockSpec(memory_space=pltpu.VMEM),
        scratch_shapes=[
            pltpu.VMEM((2, 2, CH, 7 * FINE), BF16),
            pltpu.VMEM((TAPS, FINE), F32),
            pltpu.VMEM((1, CH), jnp.int32),
            pltpu.VMEM((1, 512), jnp.int32),
            pltpu.VMEM((2, N1, N2), F32),
            pltpu.VMEM((256, 256), BF16),
            pltpu.VMEM((256, 256), BF16),
            pltpu.VMEM((256, 256), BF16),
            pltpu.VMEM((2, 512, 256), BF16),
            pltpu.VMEM((512, 512), BF16),
            pltpu.VMEM((CH, 2, HALF, 256), F32),
            pltpu.VMEM((QUARTERS, PLANE, 16, 128), BF16),
            pltpu.VMEM((QUARTERS, PLANE, 16, 128), BF16),
            pltpu.VMEM((FAR + 1, QUARTERS * DEEP, 128, 256), BF16),
            pltpu.VMEM((QUARTERS * DEEP, 256, 256), BF16),
            pltpu.VMEM((FAR + 1, 256, 128), F32),
            pltpu.VMEM((8, 128, 1024), BF16),
            pltpu.VMEM((4, 256, 256), F32),
            pltpu.VMEM((8, 2, 2, 64, 128), BF16),
            pltpu.VMEM((FAR + 1, 2, 64, 128), BF16),
            pltpu.VMEM((FAR, 2, 2, 64, 128), BF16),
            dma((2, 2)),
            dma((7,)),
            dma((QUARTERS,)),
            dma((QUARTERS,)),
            dma((QUARTERS,)),
            dma((FAR, QUARTERS * PIECES)),
            dma((FAR, QUARTERS * PIECES)),
            dma((8, 2)),
            dma((FAR + 1,)),
            dma((FAR, 2)),
        ],
        compiler_params=pltpu.CompilerParams(
            collective_id=0, has_side_effects=True, vmem_limit_bytes=60 * 2**20
        ),
        name="cross",
    )(*operands)


def local(volts, pfb_taps, channel_order, station_slot):
    order, slots = channel_order.reshape(1, CH), station_slot.reshape(1, -1)
    return cross(volts, pfb_taps, order, slots, *tables())


def solution(mesh):
    in_specs = (P(None, ("inp", "chan"), None, None), P(), P(), P())
    out_specs = P("chan", None, None, "inp", None)
    return jax.shard_map(local, mesh=mesh, in_specs=in_specs, out_specs=out_specs, check_vma=False)
```

time: 106 us -> 93.7 us (0.88)
  Pallas kernels: 99.1 us -> 89.9 us
  local copies, waits for them, and re-layouts: 6.15 us -> 2.31 us
    pallas_call x1 -> x0, Pallas kernels: 4.78 us -> none  [spectra(): pl.pallas_call(spectra_kernel, grid=(2,), out_shape=jax.ShapeDtypeStruct(...]
    pallas_call x1, Pallas kernels: 94.3 us -> 89.9 us  [cross(): pl.pallas_call(cross_kernel, out_shape=jax.ShapeDtypeStruct((1, 2, 2, 64,...]
    unnamed x17 -> x1, local copies, waits for them, and re-layouts: 6.15 us -> 2.31 us
where the time goes in v2:
time: 93.7 us; the launch traced here: 92.2 us
  Pallas kernels  89.9 us (96%)
  local copies, waits for them, and re-layouts  2.31 us (2%)
    pallas_call x1, Pallas kernels, cross(): pl.pallas_call(cross_kernel, out_shape=jax.ShapeDtypeStruct((1, 2, 2, 64,...  89.9 us
    unnamed x1, local copies, waits for them, and re-layouts  2.31 us

profile of v2, /device:TPU:6, one launch (start us, length us, event | category | flops | bytes accessed | tf_op | source)
XLA Modules:
  0.0 92.2 jit_solution(1022493960069049921)
XLA Ops:
  0.0 89.9 %cross.1 = f32[1,2,2,64,1024]{4,3,2,1,0:T(8,128)} custom-call(bf16[2,2,32,14336]{3,2,1,0:T(8,128)(2,1)} %volts_hbm.1, f32[6,2048]{1,0:T(8,128)} %taps_hbm.1, s32[1,32]{1,0:T(1,128)} %bitcast.3, s32[1,512]{1,0:T(1,128)} %bitcast.2, f32[2,16,128]{2,1,0:T(8,128)} %constant.8.clone.twiddle_hbm, bf16[256,256]{1,0:T(8,128)(2,1)} %constant.9.clone.dft_hbm, ...), custom_call_target="tpu_custom_call" | custom-call | tf_op jit(solution)/shard_map/cross/pallas_call | solution.py:433
  89.9 2.3 %copy.10 = f32[1,2,2,64,1024]{4,3,2,1,0:T(8,128)} copy(f32[1,2,2,64,1024]{4,3,2,1,0:T(8,128)} %cross.1) | data formatting | bytes 2097152

commit v3 on v2

--- a/solution.py
+++ b/solution.py
@@ -24,6 +24,7 @@
 QUARTERS = 4
 DEEP = 4
 FAR = 4
+DEPTH = 3
 PIECES = 2
 SCALE = 2.0**-22
 
@@ -93,15 +94,14 @@
     return out
 
 
-SENDS = 4
+SENDS = 2
 LATE = (FAR, FAR + 1)
+REST = 8
 ORDER = (
-    [("send", 1, n) for n in range(SENDS)]
-    + [("columns",), ("take", 0)] + [("send", 2, n) for n in range(SENDS)]
-    + [("pass", 1, 0), ("take", 1)] + [("send", 3, n) for n in range(SENDS)]
-    + [("pass", 2, 0), ("pass", 1, 1), ("pass", 2, 1)]
-    + [("take", 2), ("pass", 1, 2), ("take", 3), ("pass", 2, 2), ("pass", 1, 3), ("pass", 2, 3)]
-    + [("pass", 3, q) for q in range(QUARTERS)]
+    [("send", q, n) for q in (2, 3) for n in range(SENDS)]
+    + [("columns",), ("take", 0), ("pass", 1, 0), ("take", 1), ("pass", 2, 0), ("pass", 1, 1)]
+    + [("take", 2), ("pass", 2, 1), ("take", 3), ("pass", 1, 2), ("pass", 3, 0), ("pass", 1, 3)]
+    + [("pass", 3, 1), ("pass", 2, 2), ("pass", 2, 3), ("pass", 3, 2), ("pass", 3, 3)]
     + [("pass", 4, 0), ("pass", 4, 1), ("product",), ("pass", 4, 2), ("pass", 4, 3)]
 )
 
@@ -123,22 +123,18 @@
     def along(hops):
         return lax.rem(z + hops * way + Z, Z)
 
-    def peers(act, n=0, parts=1):
-        step = CH // 2 // parts
-        if n == 0:
-            act(1 - g, chan)
+    def peers(act, other):
+        x = 1 - g if other else g
+        act(x, lax.rem(chan + CH // 2, CH))
 
         def one(k, _):
-            for c in (lax.rem(chan + k, CH), lax.rem(chan + CH - k, CH)):
-                act(g, c)
-                act(1 - g, c)
+            act(x, lax.rem(chan + CH // 2 - k, CH))
+            act(x, lax.rem(chan + CH // 2 + k, CH))
             return 0
 
-        lax.fori_loop(max(n * step, 1), (n + 1) * step, one, 0)
-        if n == parts - 1:
-            far = lax.rem(chan + CH // 2, CH)
-            act(g, far)
-            act(1 - g, far)
+        lax.fori_loop(1, CH // 2, one, 0)
+        if other:
+            act(x, chan)
 
     small = [
         pltpu.make_async_copy(source, target, small_sem.at[n])
@@ -173,7 +169,8 @@
             )
         return 0
 
-    peers(greet)
+    peers(greet, 0)
+    peers(greet, 1)
     lax.fori_loop(1, Z, greet_column, 0)
 
     small[0].wait()
@@ -227,18 +224,18 @@
     def keep(q):
         return pltpu.make_async_copy(sent.at[q, me], arrived.at[q, me], own_sem.at[q])
 
-    def send(q, n):
+    def send(q, other):
         def one(x, c):
             pltpu.make_async_remote_copy(
                 src_ref=sent.at[q, x * CH + c],
                 dst_ref=arrived.at[q, me],
                 send_sem=turn_send.at[q],
-                recv_sem=turn_recv.at[q],
+                recv_sem=turn_recv.at[q, other],
                 device_id=(c, x * Z + z),
                 device_id_type=MESH,
             ).start()
 
-        peers(one, n, SENDS)
+        peers(one, other)
 
     def columns():
         for copy in small[4:]:
@@ -260,16 +257,37 @@
 
         lax.fori_loop(0, 8, one_hot, 0)
 
-    def pass_on(d, n):
-        several = pl.ds(n * (DEEP // PIECES), DEEP // PIECES)
+    flying = []
+
+    def forward(d, n, at):
         return pltpu.make_async_remote_copy(
-            src_ref=blocks.at[d, several],
-            dst_ref=blocks.at[d + 1, several],
+            src_ref=blocks.at[d, *at],
+            dst_ref=blocks.at[d + 1, *at],
             send_sem=ring_send.at[d, n],
             recv_sem=ring_recv.at[d, n],
             device_id=(chan, g * Z + along(1)),
             device_id_type=MESH,
         )
+
+    def launch(copy):
+        if len(flying) == DEPTH:
+            flying.pop(0).wait_send()
+        copy.start()
+        flying.append(copy)
+
+    def pass_on(d, q, n):
+        if q == 0:
+            at = (pl.ds(0, DEEP), pl.ds(pl.multiple_of(64 * (1 - g if n else g), 64), 64))
+        else:
+            at = (pl.ds(q * DEEP + n * (DEEP // PIECES), DEEP // PIECES),)
+        return forward(d, q * PIECES + n, at)
+
+    def first_of_half(q, there):
+        return q * DEEP + lax.div(there, FAR) * (DEEP // 2)
+
+    def pass_half(q, there):
+        at = (pl.ds(first_of_half(q, there), DEEP // 2),)
+        return forward(FAR - 1, q * PIECES, at)
 
     def multiply(d, start, count):
         value = None
@@ -283,12 +301,15 @@
             value = term if value is None else value + term
         total[d] += value
 
-    def take(q):
-        keep(q).wait()
-        several = arrived.at[q, pl.ds(0, PLANE - 1)]
-        pltpu.make_async_copy(several, several, turn_recv.at[q]).wait()
+    def gather(q, other):
+        x = 1 - g if other else g
+        if not other:
+            keep(q).wait()
+        several = arrived.at[q, pl.ds(0, CH if other else CH - 1)]
+        pltpu.make_async_copy(several, several, turn_recv.at[q, other]).wait()
 
         def arrange(n, _):
+            n = 2 * x + n
             rows = arrived[q, pl.ds(n * 16, 16)].reshape(256, 128)
             rows = jnp.dot(shuffle[...], rows, preferred_element_type=F32)
             rows = rows.reshape(DEEP, 2, 32, 128)
@@ -302,20 +323,33 @@
             left[several, low, :] = turned.astype(BF16).reshape(DEEP, 32, 256)
             return 0
 
-        lax.fori_loop(0, PLANE // 16, arrange, 0)
+        lax.fori_loop(0, 2, arrange, 0)
+
+    def take(q):
+        for other in range(2):
+            gather(q, other)
+            if q == 0:
+                launch(pass_on(0, q, other))
+        if q > 0:
+            for n in range(PIECES):
+                launch(pass_on(0, q, n))
+        multiply(0, q * DEEP, DEEP)
+
+    def receive(d, q):
+        if d == FAR:
+            pass_half(q, z).wait_recv()
+            multiply(d, first_of_half(q, z), DEEP // 2)
+            return
         for n in range(PIECES):
-            pass_on(0, q * PIECES + n).start()
-        multiply(0, q * DEEP, DEEP)
-
-    def receive(d, q):
-        def one(n, _):
-            pass_on(d - 1, n).wait_recv()
-            if d < FAR:
-                pass_on(d, n).start()
-            multiply(d, n * (DEEP // PIECES), DEEP // PIECES)
-            return 0
-
-        lax.fori_loop(q * PIECES, (q + 1) * PIECES, one, 0)
+            pass_on(d - 1, q, n).wait_recv()
+            if d < FAR - 1:
+                launch(pass_on(d, q, n))
+            elif n == PIECES - 1:
+                launch(pass_half(q, along(1)))
+            if q > 0:
+                multiply(d, q * DEEP + n * (DEEP // PIECES), DEEP // PIECES)
+        if q == 0:
+            multiply(d, 0, DEEP)
 
     def to_partner(d):
         return pltpu.make_async_remote_copy(
@@ -330,9 +364,9 @@
     def to_column(d, x):
         return pltpu.make_async_remote_copy(
             src_ref=mirror.at[d, x],
-            dst_ref=final.at[8 - d, g],
+            dst_ref=final.at[REST if d == FAR else 8 - d, g],
             send_sem=mirror_send.at[d, x],
-            recv_sem=final_recv.at[8 - d, g],
+            recv_sem=final_recv.at[REST if d == FAR else 8 - d, g],
             device_id=(chan, x * Z + along(-d)),
             device_id_type=MESH,
         )
@@ -344,7 +378,7 @@
             final[d, g, p] = total[d, mine, :].astype(BF16)
             partner[d, p] = total[d, other, :].astype(BF16)
         to_partner(d).start()
-        if 0 < d < FAR:
+        if d > 0:
             re = total[d, 0:128, :].T
             im = -total[d, 128:256, :].T
             for x in range(2):
@@ -354,9 +388,8 @@
 
     def placed(e, n):
         columns = slice(n * 256, (n + 1) * 256)
-        return jnp.dot(
-            final[e].reshape(256, 128), places[e, :, columns], preferred_element_type=F32
-        )
+        block = places[FAR if e == REST else e, :, columns]
+        return jnp.dot(final[e].reshape(256, 128), block, preferred_element_type=F32)
 
     def arrives(e, x):
         there = final.at[e, x]
@@ -381,8 +414,9 @@
     pl.semaphore_wait(barrier, PLANE - 1 + 2 * (Z - 1))
     for q in (0, 1):
         keep(q).start()
-    for n in range(SENDS):
-        send(0, n)
+    for q in (0, 1):
+        for n in range(SENDS):
+            send(q, n)
     spectrum(1)
     for q in (2, 3):
         keep(q).start()
@@ -401,29 +435,23 @@
             columns()
         else:
             product()
-    arrives(FAR + 1, 0)
-    arrives(FAR + 1, 1)
+    for e in (FAR + 1, REST):
+        arrives(e, 0)
+        arrives(e, 1)
     arrives(FAR, 1 - g)
     for n in range(4):
-        tile = (sums[n] + placed(FAR + 1, n) + placed(FAR, n)) * SCALE
+        tile = (sums[n] + placed(FAR + 1, n) + placed(FAR, n) + placed(REST, n)) * SCALE
         out[0, :, :, :, n * 256 : (n + 1) * 256] = tile.reshape(2, 2, 64, 256)
 
     for q in range(QUARTERS):
         several = sent.at[q, pl.ds(0, PLANE - 1)]
         pltpu.make_async_copy(several, several, turn_send.at[q]).wait()
 
-    def drain(d, _):
-        def one(n, _):
-            pass_on(d, n).wait_send()
-            return 0
-
-        lax.fori_loop(0, QUARTERS * PIECES, one, 0)
-        return 0
-
-    lax.fori_loop(0, FAR, drain, 0)
+    for copy in flying:
+        copy.wait_send()
     for d in range(FAR + 1):
         to_partner(d).wait_send()
-        if 0 < d < FAR:
+        if d > 0:
             for x in range(2):
                 to_column(d, x).wait_send()
 
@@ -454,19 +482,19 @@
             pltpu.VMEM((FAR + 1, 256, 128), F32),
             pltpu.VMEM((8, 128, 1024), BF16),
             pltpu.VMEM((4, 256, 256), F32),
-            pltpu.VMEM((8, 2, 2, 64, 128), BF16),
+            pltpu.VMEM((9, 2, 2, 64, 128), BF16),
             pltpu.VMEM((FAR + 1, 2, 64, 128), BF16),
-            pltpu.VMEM((FAR, 2, 2, 64, 128), BF16),
+            pltpu.VMEM((FAR + 1, 2, 2, 64, 128), BF16),
             dma((2, 2)),
             dma((7,)),
             dma((QUARTERS,)),
             dma((QUARTERS,)),
-            dma((QUARTERS,)),
+            dma((QUARTERS, 2)),
             dma((FAR, QUARTERS * PIECES)),
             dma((FAR, QUARTERS * PIECES)),
-            dma((8, 2)),
+            dma((9, 2)),
             dma((FAR + 1,)),
-            dma((FAR, 2)),
+            dma((FAR + 1, 2)),
         ],
         compiler_params=pltpu.CompilerParams(
             collective_id=0, has_side_effects=True, vmem_limit_bytes=60 * 2**20

time: 93.7 us -> 86.5 us (0.923); the launches traced: 92.2 us -> 86.3 us
  Pallas kernels: 89.9 us -> 84 us
    pallas_call x1, Pallas kernels: 89.9 us -> 84 us  [cross(): pl.pallas_call(cross_kernel, out_shape=jax.ShapeDtypeStruct((1, 2, 2, 64,...]
where the time goes in v3:
time: 86.5 us; the launch traced here: 86.3 us
  Pallas kernels  84 us (97%)
  local copies, waits for them, and re-layouts  2.31 us (3%)
    pallas_call x1, Pallas kernels, cross(): pl.pallas_call(cross_kernel, out_shape=jax.ShapeDtypeStruct((1, 2, 2, 64,...  84 us
    unnamed x1, local copies, waits for them, and re-layouts  2.31 us

profile of v3, /device:TPU:6, one launch (start us, length us, event | category | flops | bytes accessed | tf_op | source)
XLA Modules:
  0.0 86.3 jit_solution(4601551699634151788)
XLA Ops:
  0.0 84.0 %cross.1 = f32[1,2,2,64,1024]{4,3,2,1,0:T(8,128)} custom-call(bf16[2,2,32,14336]{3,2,1,0:T(8,128)(2,1)} %volts_hbm.1, f32[6,2048]{1,0:T(8,128)} %taps_hbm.1, s32[1,32]{1,0:T(1,128)} %bitcast.3, s32[1,512]{1,0:T(1,128)} %bitcast.2, f32[2,16,128]{2,1,0:T(8,128)} %constant.8.clone.twiddle_hbm, bf16[256,256]{1,0:T(8,128)(2,1)} %constant.9.clone.dft_hbm, ...), custom_call_target="tpu_custom_call" | custom-call | tf_op jit(solution)/shard_map/cross/pallas_call | solution.py:461
  84.0 2.3 %copy.10 = f32[1,2,2,64,1024]{4,3,2,1,0:T(8,128)} copy(f32[1,2,2,64,1024]{4,3,2,1,0:T(8,128)} %cross.1) | data formatting | bytes 2097152

commit v4 on v3

--- a/solution.py
+++ b/solution.py
@@ -95,7 +95,7 @@
 
 
 SENDS = 2
-LATE = (FAR, FAR + 1)
+LATE = (FAR - 1, FAR, FAR + 1)
 REST = 8
 ORDER = (
     [("send", q, n) for q in (2, 3) for n in range(SENDS)]
@@ -275,10 +275,14 @@
         copy.start()
         flying.append(copy)
 
-    def pass_on(d, q, n):
-        if q == 0:
+    def turned_round(d, n):
+        return lax.rem(n + lax.div(along(FAR - d), FAR), PIECES)
+
+    def pass_on(d, q, n, came):
+        if q == 0 and d < FAR - 2:
             at = (pl.ds(0, DEEP), pl.ds(pl.multiple_of(64 * (1 - g if n else g), 64), 64))
         else:
+            n = turned_round(came, n)
             at = (pl.ds(q * DEEP + n * (DEEP // PIECES), DEEP // PIECES),)
         return forward(d, q * PIECES + n, at)
 
@@ -329,10 +333,10 @@
         for other in range(2):
             gather(q, other)
             if q == 0:
-                launch(pass_on(0, q, other))
+                launch(pass_on(0, q, other, 0))
         if q > 0:
             for n in range(PIECES):
-                launch(pass_on(0, q, n))
+                launch(pass_on(0, q, n, 0))
         multiply(0, q * DEEP, DEEP)
 
     def receive(d, q):
@@ -341,14 +345,19 @@
             multiply(d, first_of_half(q, z), DEEP // 2)
             return
         for n in range(PIECES):
-            pass_on(d - 1, q, n).wait_recv()
-            if d < FAR - 1:
-                launch(pass_on(d, q, n))
-            elif n == PIECES - 1:
-                launch(pass_half(q, along(1)))
+            pass_on(d - 1, q, n, d).wait_recv()
+            if d == FAR - 1:
+                if n == 0:
+                    launch(pass_half(q, along(1)))
+            elif q > 0 or d < FAR - 2:
+                launch(pass_on(d, q, n, d))
             if q > 0:
-                multiply(d, q * DEEP + n * (DEEP // PIECES), DEEP // PIECES)
+                first_of_piece = q * DEEP + turned_round(d, n) * (DEEP // PIECES)
+                multiply(d, first_of_piece, DEEP // PIECES)
         if q == 0:
+            if d == FAR - 2:
+                for n in range(PIECES):
+                    launch(pass_on(d, q, n, d))
             multiply(d, 0, DEEP)
 
     def to_partner(d):
@@ -372,12 +381,6 @@
         )
 
     def finish(d):
-        for p in range(2):
-            mine = pl.ds(pl.multiple_of(p * 128 + g * 64, 64), 64)
-            other = pl.ds(pl.multiple_of(p * 128 + (1 - g) * 64, 64), 64)
-            final[d, g, p] = total[d, mine, :].astype(BF16)
-            partner[d, p] = total[d, other, :].astype(BF16)
-        to_partner(d).start()
         if d > 0:
             re = total[d, 0:128, :].T
             im = -total[d, 128:256, :].T
@@ -385,6 +388,12 @@
                 mirror[d, x, 0] = re[x * 64 : (x + 1) * 64].astype(BF16)
                 mirror[d, x, 1] = im[x * 64 : (x + 1) * 64].astype(BF16)
                 to_column(d, x).start()
+        for p in range(2):
+            mine = pl.ds(pl.multiple_of(p * 128 + g * 64, 64), 64)
+            other = pl.ds(pl.multiple_of(p * 128 + (1 - g) * 64, 64), 64)
+            final[d, g, p] = total[d, mine, :].astype(BF16)
+            partner[d, p] = total[d, other, :].astype(BF16)
+        to_partner(d).start()
 
     def placed(e, n):
         columns = slice(n * 256, (n + 1) * 256)
@@ -397,7 +406,7 @@
 
     def product():
         for e in range(8):
-            if e < FAR:
+            if e < FAR - 1:
                 arrives(e, 1 - g)
             if e > FAR + 1:
                 arrives(e, 0)
@@ -435,13 +444,17 @@
             columns()
         else:
             product()
-    for e in (FAR + 1, REST):
-        arrives(e, 0)
-        arrives(e, 1)
+    arrives(FAR - 1, 1 - g)
+    arrives(FAR + 1, 0)
+    arrives(FAR + 1, 1)
     arrives(FAR, 1 - g)
     for n in range(4):
-        tile = (sums[n] + placed(FAR + 1, n) + placed(FAR, n) + placed(REST, n)) * SCALE
-        out[0, :, :, :, n * 256 : (n + 1) * 256] = tile.reshape(2, 2, 64, 256)
+        sums[n] += placed(FAR - 1, n) + placed(FAR + 1, n) + placed(FAR, n)
+    arrives(REST, 0)
+    arrives(REST, 1)
+    for n in range(4):
+        tile = sums[n] + placed(REST, n)
+        out[0, :, :, :, n * 256 : (n + 1) * 256] = tile.astype(BF16).reshape(2, 2, 64, 256)
 
     for q in range(QUARTERS):
         several = sent.at[q, pl.ds(0, PLANE - 1)]
@@ -460,7 +473,7 @@
     dma = pltpu.SemaphoreType.DMA
     return pl.pallas_call(
         cross_kernel,
-        out_shape=jax.ShapeDtypeStruct((1, 2, 2, 64, 1024), F32),
+        out_shape=jax.ShapeDtypeStruct((1, 2, 2, 64, 1024), BF16),
         in_specs=[pl.BlockSpec(memory_space=pl.ANY)] * 8,
         out_specs=pl.BlockSpec(memory_space=pltpu.VMEM),
         scratch_shapes=[
@@ -505,7 +518,7 @@
 
 def local(volts, pfb_taps, channel_order, station_slot):
     order, slots = channel_order.reshape(1, CH), station_slot.reshape(1, -1)
-    return cross(volts, pfb_taps, order, slots, *tables())
+    return cross(volts, pfb_taps, order, slots, *tables()).astype(F32) * SCALE
 
 
 def solution(mesh):

time: 86.5 us -> 85.1 us (0.984)
  local copies, waits for them, and re-layouts: 2.31 us -> 0 us
  other arithmetic: 0 us -> 2.13 us
  Pallas kernels: 84 us -> 82.2 us
    unnamed x1 -> x0, local copies, waits for them, and re-layouts: 2.31 us -> none
    mul x0 -> x1, other arithmetic: none -> 2.13 us  [local(): return cross(volts, pfb_taps, order, slots, *tables()).astype(F32) * SCALE]
    pallas_call x1, Pallas kernels: 84 us -> 82.2 us  [cross(): pl.pallas_call(cross_kernel, out_shape=jax.ShapeDtypeStruct((1, 2, 2, 64,...]
where the time goes in v4:
time: 85.1 us; the launch traced here: 84.3 us
  Pallas kernels  82.2 us (97%)
  other arithmetic  2.13 us (3%)
    pallas_call x1, Pallas kernels, cross(): pl.pallas_call(cross_kernel, out_shape=jax.ShapeDtypeStruct((1, 2, 2, 64,...  82.2 us
    mul x1, other arithmetic, local(): return cross(volts, pfb_taps, order, slots, *tables()).astype(F32) * SCALE  2.13 us

profile of v4, /device:TPU:6, one launch (start us, length us, event | category | flops | bytes accessed | tf_op | source)
XLA Modules:
  0.0 84.3 jit_solution(3504141094751158876)
XLA Ops:
  0.0 82.2 %cross.1 = bf16[1,2,2,64,1024]{4,3,2,1,0:T(8,128)(2,1)} custom-call(bf16[2,2,32,14336]{3,2,1,0:T(8,128)(2,1)} %volts_hbm.1, f32[6,2048]{1,0:T(8,128)} %taps_hbm.1, s32[1,32]{1,0:T(1,128)} %bitcast.3, s32[1,512]{1,0:T(1,128)} %bitcast.2, f32[2,16,128]{2,1,0:T(8,128)} %constant.10.clone.twiddle_hbm, bf16[256,256]{1,0:T(8,128)(2,1)} %constant.11.clone.dft_hbm, ...), custom_call_target="tpu_custom_call" | custom-call | tf_op jit(solution)/shard_map/cross/pallas_call | solution.py:474
  82.2 2.1 %convert_multiply_fusion = f32[1,2,2,64,1024]{4,3,2,1,0:T(8,128)} fusion(bf16[1,2,2,64,1024]{4,3,2,1,0:T(8,128)(2,1)} %cross.1), kind=kLoop, calls=%fused_computation | loop fusion | flops 524288 | bytes 1572864 | tf_op jit(solution)/shard_map/mul | solution.py:521

commit v5 on v4

--- a/solution.py
+++ b/solution.py
@@ -95,7 +95,7 @@
 
 
 SENDS = 2
-LATE = (FAR - 1, FAR, FAR + 1)
+LATE = (FAR - 1, FAR, FAR + 1, FAR + 2)
 REST = 8
 ORDER = (
     [("send", q, n) for q in (2, 3) for n in range(SENDS)]
@@ -387,7 +387,8 @@
             for x in range(2):
                 mirror[d, x, 0] = re[x * 64 : (x + 1) * 64].astype(BF16)
                 mirror[d, x, 1] = im[x * 64 : (x + 1) * 64].astype(BF16)
-                to_column(d, x).start()
+            to_column(d, 1 - g).start()
+            to_column(d, g).start()
         for p in range(2):
             mine = pl.ds(pl.multiple_of(p * 128 + g * 64, 64), 64)
             other = pl.ds(pl.multiple_of(p * 128 + (1 - g) * 64, 64), 64)
@@ -408,7 +409,7 @@
         for e in range(8):
             if e < FAR - 1:
                 arrives(e, 1 - g)
-            if e > FAR + 1:
+            if e > FAR + 2:
                 arrives(e, 0)
                 arrives(e, 1)
         for n in range(4):
@@ -445,11 +446,13 @@
         else:
             product()
     arrives(FAR - 1, 1 - g)
-    arrives(FAR + 1, 0)
-    arrives(FAR + 1, 1)
+    for e in (FAR + 2, FAR + 1):
+        arrives(e, 0)
+        arrives(e, 1)
     arrives(FAR, 1 - g)
     for n in range(4):
-        sums[n] += placed(FAR - 1, n) + placed(FAR + 1, n) + placed(FAR, n)
+        for e in LATE:
+            sums[n] += placed(e, n)
     arrives(REST, 0)
     arrives(REST, 1)
     for n in range(4):

time: 85.1 us -> 85.1 us (level)
  no operation moved by 1% of the time
where the time goes in v5:
time: 85.1 us; the launch traced here: 84 us
  Pallas kernels  81.9 us (96%)
  other arithmetic  2.13 us (3%)
    pallas_call x1, Pallas kernels, cross(): pl.pallas_call(cross_kernel, out_shape=jax.ShapeDtypeStruct((1, 2, 2, 64,...  81.9 us
    mul x1, other arithmetic, local(): return cross(volts, pfb_taps, order, slots, *tables()).astype(F32) * SCALE  2.13 us

profile of v5, /device:TPU:6, one launch (start us, length us, event | category | flops | bytes accessed | tf_op | source)
XLA Modules:
  0.0 84.0 jit_solution(9437398878407458829)
XLA Ops:
  0.0 81.9 %cross.1 = bf16[1,2,2,64,1024]{4,3,2,1,0:T(8,128)(2,1)} custom-call(bf16[2,2,32,14336]{3,2,1,0:T(8,128)(2,1)} %volts_hbm.1, f32[6,2048]{1,0:T(8,128)} %taps_hbm.1, s32[1,32]{1,0:T(1,128)} %bitcast.3, s32[1,512]{1,0:T(1,128)} %bitcast.2, f32[2,16,128]{2,1,0:T(8,128)} %constant.10.clone.twiddle_hbm, bf16[256,256]{1,0:T(8,128)(2,1)} %constant.11.clone.dft_hbm, ...), custom_call_target="tpu_custom_call" | custom-call | tf_op jit(solution)/shard_map/cross/pallas_call | solution.py:477
  81.9 2.1 %convert_multiply_fusion = f32[1,2,2,64,1024]{4,3,2,1,0:T(8,128)} fusion(bf16[1,2,2,64,1024]{4,3,2,1,0:T(8,128)(2,1)} %cross.1), kind=kLoop, calls=%fused_computation | loop fusion | flops 524288 | bytes 1572864 | tf_op jit(solution)/shard_map/mul | solution.py:524
